TPU v7x, 512 devices: a whole 4x4x16 slice. The times are simulated.
512 devices in a mesh: replica: 32 (over x, y, z_hi), fsdp: 16 (over z_lo, core).
Axes of the slice: x: 4, y: 4, z: 16 (z_hi: 2, z_lo: 8; z = z_hi * 8 + z_lo), core: 2. Of those that a mesh axis runs over, the one named last changes fastest.
Arguments:
- tokens: bfloat16 [98304, 4096], P(('replica', 'fsdp')), may hold values from -6 to 6
- grads_out: bfloat16 [98304, 1024], P(('replica', 'fsdp')), may hold values from -6 to 6
- weights: bfloat16 [32, 4096, 1024], P('replica', 'fsdp'), may hold values from -0.29882812 to 0.29882812
- moments: float32 [32, 4096, 1024], P('replica', 'fsdp'), may hold values from -6 to 6
- step: int32 [1], replicated, may hold values from 0 to 999
Outputs:
- mixed_weights: bfloat16 [32, 4096, 1024], P('replica', 'fsdp')
- new_moments: float32 [32, 4096, 1024], P('replica', 'fsdp')
All inputs are finite; a program needn't handle non-finite values.
Results may differ from a plain program's by a relative error of at most 0.001.
Values may be sent and summed in bfloat16 or wider, within the bound.
A program may use at most 64 MiB of HBM per device.

v0:
```python
import functools

import jax
import jax.numpy as jnp
from jax import lax
from jax.experimental import pallas as pl
from jax.experimental.pallas import tpu as pltpu
from jax.sharding import PartitionSpec as P

MESH = pl.DeviceIdType.MESH
TOP = 32767.0
TINY = 1e-30
HOP = 2
LANES = 256
GROUP = 256


def kernel(
    replicas,
    chips,
    distance,
    scale,
    tokens_hbm,
    grads_hbm,
    weights_hbm,
    moments_hbm,
    mixed_hbm,
    new_hbm,
    tok,
    grad,
    edge_tok,
    edge_grad,
    buf,
    factor,
    part,
    weights,
    moments,
    new,
    updated,
    mixed,
    out_buf,
    out_factor,
    in_buf,
    in_factor,
    own_sem,
    sib_send,
    sib_recv,
    own_grad_sem,
    sib_grad_send,
    sib_grad_recv,
    load_sem,
    edge_send,
    edge_recv,
    edge_grad_send,
    edge_grad_recv,
    pass_send,
    pass_recv,
    send,
    recv,
    factor_send,
    factor_recv,
    gossip_send,
    gossip_recv,
    gossip_factor_send,
    gossip_factor_recv,
    new_sem,
    mixed_sem,
):
    last = chips - 1
    units, features, width = updated.shape
    replica = lax.axis_index("replica")
    me = lax.axis_index("fsdp")
    chip = me // 2
    core = me % 2
    sibling = chip * 2 + 1 - core
    left = jnp.maximum(me - 2, 0)
    right = jnp.minimum(me + 2, 2 * chips - 1)
    partner = (replica + distance) % replicas
    source = (replica + replicas - distance) % replicas
    at_end = jnp.logical_or(chip == 0, chip == last)
    next_to_end = jnp.logical_or(chip == 1, chip == last - 1)
    high = chip >= chips // 2
    inner = jnp.where(high, last - 1, 1)
    outer = jnp.where(high, last, 0)

    def span(unit):
        return pl.ds(pl.multiple_of(unit * width, width), width)

    def remote(source_ref, to_ref, send_sem, recv_sem, device):
        return pltpu.make_async_remote_copy(
            src_ref=source_ref,
            dst_ref=to_ref,
            send_sem=send_sem,
            recv_sem=recv_sem,
            device_id=device,
            device_id_type=MESH,
        )

    def piece(target, which):
        start = pl.multiple_of((2 * target + which) * features, features)
        return tokens_hbm.at[:, pl.ds(start, features)]

    def own_copy(target):
        return pltpu.make_async_copy(piece(target, core), tok.at[target, core], own_sem.at[target])

    def sibling_copy(target):
        return remote(
            piece(target, 1 - core),
            tok.at[target, core],
            sib_send.at[target],
            sib_recv.at[target],
            {"fsdp": sibling},
        )

    def own_grad(unit):
        return pltpu.make_async_copy(
            grads_hbm.at[:, span(unit)], grad.at[unit, core], own_grad_sem.at[unit]
        )

    def sibling_grad(unit):
        return remote(
            grads_hbm.at[:, span(unit)],
            grad.at[unit, core],
            sib_grad_send.at[unit],
            sib_grad_recv.at[unit],
            {"fsdp": sibling},
        )

    def edge_target(rank):
        return jnp.where(high, rank, last - rank)

    def edge_copy(rank, which):
        return remote(
            piece(edge_target(rank), which),
            edge_tok.at[rank, core],
            edge_send.at[rank, which],
            edge_recv.at[rank, core],
            {"fsdp": inner * 2 + which},
        )

    def edge_arrival(rank, which):
        return remote(
            edge_tok.at[rank, which],
            edge_tok.at[rank, which],
            edge_send.at[rank, which],
            edge_recv.at[rank, which],
            {"fsdp": sibling},
        )

    def edge_grad_copy(unit):
        return remote(
            grads_hbm.at[:, span(unit)],
            edge_grad.at[unit, core],
            edge_grad_send.at[unit],
            edge_grad_recv.at[unit],
            {"fsdp": inner * 2 + core},
        )

    def edge_grad_arrival(unit):
        return remote(
            edge_grad.at[unit, core],
            edge_grad.at[unit, core],
            edge_grad_send.at[unit],
            edge_grad_recv.at[unit],
            {"fsdp": sibling},
        )

    def pass_copy(unit, which):
        return remote(
            edge_grad.at[unit, which],
            edge_grad.at[unit, which],
            pass_send.at[unit],
            pass_recv.at[unit],
            {"fsdp": sibling},
        )

    def load(unit):
        return (
            pltpu.make_async_copy(
                weights_hbm.at[0, :, span(unit)], weights.at[unit], load_sem.at[0, unit]
            ),
            pltpu.make_async_copy(
                moments_hbm.at[0, :, span(unit)], moments.at[unit], load_sem.at[1, unit]
            ),
        )

    def hop(way, slot):
        device = {"fsdp": left if way == 0 else right}
        return (
            remote(
                buf.at[way, slot],
                buf.at[way, slot],
                send.at[way, slot],
                recv.at[way, slot],
                device,
            ),
            remote(
                factor.at[way, slot],
                factor.at[way, slot],
                factor_send.at[way, slot],
                factor_recv.at[way, slot],
                device,
            ),
        )

    def gossip(unit):
        device = {"replica": partner}
        return (
            remote(
                out_buf.at[unit],
                in_buf.at[unit],
                gossip_send.at[unit],
                gossip_recv.at[unit],
                device,
            ),
            remote(
                out_factor.at[unit],
                in_factor.at[unit],
                gossip_factor_send.at[unit],
                gossip_factor_recv.at[unit],
                device,
            ),
        )

    def new_copy(unit):
        return pltpu.make_async_copy(new.at[unit], new_hbm.at[0, :, span(unit)], new_sem.at[unit])

    def mixed_copy(unit):
        return pltpu.make_async_copy(
            mixed.at[unit], mixed_hbm.at[0, :, span(unit)], mixed_sem.at[unit]
        )

    order = []
    for near in range(chips // 2):
        order += [near, last - near]

    barrier = pltpu.get_barrier_semaphore()
    pl.semaphore_signal(barrier, inc=1, device_id={"fsdp": sibling}, device_id_type=MESH)
    pl.semaphore_signal(barrier, inc=1, device_id={"replica": source}, device_id_type=MESH)

    @pl.when(chip > 0)
    def _():
        pl.semaphore_signal(barrier, inc=1, device_id={"fsdp": left}, device_id_type=MESH)

    @pl.when(chip < last)
    def _():
        pl.semaphore_signal(barrier, inc=1, device_id={"fsdp": right}, device_id_type=MESH)

    @pl.when(next_to_end)
    def _():
        pl.semaphore_signal(
            barrier, inc=1, device_id={"fsdp": outer * 2 + 1 - core}, device_id_type=MESH
        )

    for unit in range(units):
        own_grad(unit).start()
    def needs(target):
        return jnp.logical_or(jnp.logical_not(at_end), chip == target)

    for target in order:

        @pl.when(needs(target))
        def _(target=target):
            own_copy(target).start()

    pl.semaphore_wait(barrier, 4)

    @pl.when(at_end)
    def _():
        edge_grad_copy(0).start()
        edge_copy(0, 0).start()
        edge_copy(0, 1).start()

    for unit in range(units):
        sibling_grad(unit).start()
    for target in order:

        @pl.when(needs(target))
        def _(target=target):
            sibling_copy(target).start()

    @pl.when(at_end)
    def _():
        for unit in range(1, units):
            edge_grad_copy(unit).start()
        for rank in range(1, last):
            edge_copy(rank, 0).start()
            edge_copy(rank, 1).start()

    for unit in range(units):
        for copy in load(unit):
            copy.start()

    for unit in range(units):
        own_grad(unit).wait()
        sibling_grad(unit).wait_recv()

    def dot(a, b):
        return lax.dot_general(
            a.reshape(-1, a.shape[-1]),
            b.reshape(-1, b.shape[-1]),
            (((0,), (0,)), ((), ())),
            preferred_element_type=jnp.float32,
        )

    def decode(data, factors):
        return data.astype(jnp.int32).astype(jnp.float32) * factors

    def encode(value):
        largest = jnp.max(jnp.abs(value), axis=0, keepdims=True)
        largest = jnp.maximum(largest, TINY)
        code = jnp.round(value * (TOP / largest * (1.0 - 1e-6)))
        return code.astype(jnp.int32).astype(jnp.int16), largest * (1.0 / TOP / (1.0 - 1e-6))

    groups = [(g, slice(g * GROUP, (g + 1) * GROUP)) for g in range(features // GROUP)]

    def multiply(slot, target, rank, unit, with_edge):
        @pl.when(unit == 0)
        def _():
            own_copy(target).wait()
            sibling_copy(target).wait_recv()

        part[slot] = dot(tok[target], grad[unit])

        @pl.when(with_edge)
        def _():
            @pl.when(rank == 0)
            def _():
                edge_grad_arrival(unit).wait_recv()
                pass_copy(unit, core).start()
                pass_copy(unit, 1 - core).wait_recv()

            @pl.when(unit == 0)
            def _():
                edge_arrival(rank, 0).wait_recv()
                edge_arrival(rank, 1).wait_recv()

            part[slot] += dot(edge_tok[rank], edge_grad[unit])

    def receive(slot, way, at):
        for copy in hop(way, at):
            copy.wait_recv()
        for g, rows in groups:
            part[slot, rows] += decode(buf[way, at, rows], factor[way, at, g : g + 1])

    def forward(way, at, beside_end):
        rank = at // units
        multiply(way, rank if way == 0 else last - rank, rank, at % units, beside_end)

        @pl.when(jnp.logical_not(beside_end))
        def _():
            receive(way, way, at)

        for g, rows in groups:
            buf[way, at, rows], factor[way, at, g : g + 1] = encode(part[way, rows])
        for copy in hop(way, at):
            copy.start()

    from_right = chip * units
    from_left = (last - chip) * units
    lag_right = jnp.maximum(last - 1 - chip, 0) * HOP
    lag_left = jnp.maximum(chip - 1, 0) * HOP
    largest_slot = (last - 1) * units - 1

    def finish(unit):
        multiply(2, chip, last - 1, unit, next_to_end)

        @pl.when(chip < last - 1)
        def _():
            receive(2, 0, jnp.minimum(from_right + unit, largest_slot))

        @pl.when(chip > 1)
        def _():
            receive(2, 1, jnp.minimum(from_left + unit, largest_slot))

        for copy in load(unit):
            copy.wait()
        for g, rows in groups:
            moment = 0.9 * moments[unit, rows] + part[2, rows] * scale
            new[unit, rows] = moment
            value = weights[unit, rows].astype(jnp.float32) - 0.05 * moment
            updated[unit, rows] = value
            out_buf[unit, rows], out_factor[unit, g : g + 1] = encode(value)
        for copy in gossip(unit):
            copy.start()
        new_copy(unit).start()

    begin_finish = jnp.maximum(
        jnp.where(chip < last, from_right + lag_right, 0),
        jnp.where(chip > 0, from_left + lag_left, 0),
    )

    def step(i, carry):
        at_l = i - lag_right
        at_r = i - lag_left
        unit = i - begin_finish

        @pl.when((at_l >= 0) & (at_l < from_right) & (chip < last))
        def _():
            forward(0, at_l, chip == last - 1)

        @pl.when((at_r >= 0) & (at_r < from_left) & (chip > 0))
        def _():
            forward(1, at_r, chip == 1)

        @pl.when((unit >= 0) & (unit < units))
        def _():
            finish(unit)

        return carry

    steps = (last - 1) * max(units, HOP) + units + HOP
    lax.fori_loop(0, steps, step, 0)

    def mix(unit, carry):
        for copy in gossip(unit):
            copy.wait_recv()
        for g, rows in groups:
            theirs = decode(in_buf[unit, rows], in_factor[unit, g : g + 1])
            mixed[unit, rows] = ((updated[unit, rows] + theirs) * 0.5).astype(jnp.bfloat16)
        mixed_copy(unit).start()
        return carry

    lax.fori_loop(0, units, mix, 0)

    def drain_left(at, carry):
        for copy in hop(0, at):
            copy.wait_send()
        return carry

    def drain_right(at, carry):
        for copy in hop(1, at):
            copy.wait_send()
        return carry

    lax.fori_loop(0, jnp.where(chip < last, from_right, 0), drain_left, 0)
    lax.fori_loop(0, jnp.where(chip > 0, from_left, 0), drain_right, 0)

    @pl.when(at_end)
    def _():
        for unit in range(units):
            edge_grad_copy(unit).wait_send()
        for rank in range(last):
            edge_copy(rank, 0).wait_send()
            edge_copy(rank, 1).wait_send()

    @pl.when(next_to_end)
    def _():
        for unit in range(units):
            pass_copy(unit, core).wait_send()

    for unit in range(units):
        sibling_grad(unit).wait_send()
    for target in range(chips):

        @pl.when(needs(target))
        def _(target=target):
            sibling_copy(target).wait_send()

    def drain(unit, carry):
        for copy in gossip(unit):
            copy.wait_send()
        new_copy(unit).wait()
        mixed_copy(unit).wait()
        return carry

    lax.fori_loop(0, units, drain, 0)


def step_with(level, replicas, members, tokens, grads_out, weights, moments):
    chips = members // 2
    last = chips - 1
    held = tokens.shape[0]
    columns = grads_out.shape[1]
    features = weights.shape[1]
    width = min(LANES, columns)
    units = columns // width
    groups = features // GROUP
    passed = (last - 1) * units
    dma = pltpu.SemaphoreType.DMA
    return pl.pallas_call(
        functools.partial(kernel, replicas, chips, 1 << level, float((held * members) ** -0.5)),
        out_shape=(
            jax.ShapeDtypeStruct(weights.shape, jnp.bfloat16),
            jax.ShapeDtypeStruct(moments.shape, jnp.float32),
        ),
        in_specs=[pl.BlockSpec(memory_space=pl.ANY)] * 4,
        out_specs=[pl.BlockSpec(memory_space=pl.ANY)] * 2,
        scratch_shapes=[
            pltpu.VMEM((chips, 2, held, features), jnp.bfloat16),
            pltpu.VMEM((units, 2, held, width), jnp.bfloat16),
            pltpu.VMEM((last, 2, held, features), jnp.bfloat16),
            pltpu.VMEM((units, 2, held, width), jnp.bfloat16),
            pltpu.VMEM((2, passed, features, width), jnp.int16),
            pltpu.VMEM((2, passed, groups, width), jnp.float32),
            pltpu.VMEM((3, features, width), jnp.float32),
            pltpu.VMEM((units, features, width), jnp.bfloat16),
            pltpu.VMEM((units, features, width), jnp.float32),
            pltpu.VMEM((units, features, width), jnp.float32),
            pltpu.VMEM((units, features, width), jnp.float32),
            pltpu.VMEM((units, features, width), jnp.bfloat16),
            pltpu.VMEM((units, features, width), jnp.int16),
            pltpu.VMEM((units, groups, width), jnp.float32),
            pltpu.VMEM((units, features, width), jnp.int16),
            pltpu.VMEM((units, groups, width), jnp.float32),
            dma((chips,)),
            dma((chips,)),
            dma((chips,)),
            dma((units,)),
            dma((units,)),
            dma((units,)),
            dma((2, units)),
            dma((last, 2)),
            dma((last, 2)),
            dma((units,)),
            dma((units,)),
            dma((units,)),
            dma((units,)),
            dma((2, passed)),
            dma((2, passed)),
            dma((2, passed)),
            dma((2, passed)),
            dma((units,)),
            dma((units,)),
            dma((units,)),
            dma((units,)),
            dma((units,)),
            dma((units,)),
        ],
        compiler_params=pltpu.CompilerParams(
            collective_id=level, has_side_effects=True, vmem_limit_bytes=44 * 1024 * 1024
        ),
        cost_estimate=pl.CostEstimate(
            flops=2 * held * members * features * columns,
            bytes_accessed=2 * tokens.size + 10 * features * columns,
            transcendentals=0,
        ),
    )(tokens, grads_out, weights, moments)


def solution(mesh):
    replicas, members = mesh.shape["replica"], mesh.shape["fsdp"]
    levels = replicas.bit_length() - 1

    def body(tokens, grads_out, weights, moments, step):
        level = step[0] % levels
        branches = [
            functools.partial(step_with, power, replicas, members) for power in range(levels)
        ]
        return lax.switch(level, branches, tokens, grads_out, weights, moments)

    return jax.shard_map(
        body,
        mesh=mesh,
        in_specs=(
            P(("replica", "fsdp"), None),
            P(("replica", "fsdp"), None),
            P("replica", "fsdp", None),
            P("replica", "fsdp", None),
            P(),
        ),
        out_specs=(P("replica", "fsdp", None), P("replica", "fsdp", None)),
        check_vma=False,
    )
```

profile of v0, /device:TPU:64, one launch (start us, length us, event | category | flops | bytes accessed | tf_op | source)
XLA Modules:
  0.0 97.0 jit_solution(11276777287267518638)
XLA Ops:
  1.3 93.9 %conditional.1 = ((bf16[1,256,1024]{2,1,0:T(8,128)(2,1)S(1)}, f32[1,256,1024]{2,1,0:T(8,128)S(1)})) conditional(s32[]{:T(128)} %clamp.3, (bf16[192,4096]{1,0:T(8,128)(2,1)}, bf16[192,1024]{1,0:T(8,128)(2,1)}, bf16[1,256,1024]{2,1,0:T(8,128)(2,1)}, f32[1,256,1024]{2,1,0:T(8,128)}) %tuple.22, ...), branch_computations={%region_0.1_spmd, %region_1.2_spmd, %region_2.3_spmd, %region_3.4_... | conditional | flops 1610612736 | bytes 4194312 | solution.py:550
  1.3 93.9 %branch_3_fun.1 = (bf16[1,256,1024]{2,1,0:T(8,128)(2,1)S(1)}, f32[1,256,1024]{2,1,0:T(8,128)S(1)}) custom-call(bf16[192,4096]{1,0:T(8,128)(2,1)} %get-tuple-element.52.tokens_hbm, bf16[192,1024]{1,0:T(8,128)(2,1)} %get-tuple-element.53.grads_hbm, bf16[1,256,1024]{2,1,0:T(8,128)(2,1)} %get-tuple-element.54.weights_hbm, ...), custom_call_target="tpu_custom_call" | custom-call | flops 1610612736 | bytes 4194304 | tf_op jit(solution)/shard_map/cond/branch_3_fun/pallas_call | solution.py:481
  95.2 0.8 copy.30
  96.0 1.0 copy.31
where the time goes:
time: 97.1 us; the launch traced here: 97 us
  Pallas kernels  93.9 us (97%)
  local copies, waits for them, and re-layouts  1.77 us (2%)
  between operations  1.3 us (1%)
    pallas_call x1, Pallas kernels, step_with(): pl.pallas_call(functools.partial(kernel, replicas, chips, 1 << level, flo...  93.9 us

commit v1 on v0

--- a/solution.py
+++ b/solution.py
@@ -12,7 +12,6 @@
 TINY = 1e-30
 HOP = 2
 LANES = 256
-GROUP = 256
 
 
 def kernel(
@@ -59,6 +58,8 @@
     recv,
     factor_send,
     factor_recv,
+    half_send,
+    half_recv,
     gossip_send,
     gossip_recv,
     gossip_factor_send,
@@ -184,50 +185,69 @@
             ),
         )
 
-    def hop(way, slot):
-        device = {"fsdp": left if way == 0 else right}
+    half = features // 2
+
+    def half_rows(part_of):
+        return pl.ds(pl.multiple_of(part_of * half, half), half)
+
+    def hop_whole(way, slot):
+        return remote(
+            buf.at[way, slot],
+            buf.at[way, slot],
+            send.at[way, slot],
+            recv.at[way, slot],
+            {"fsdp": left if way == 0 else right},
+        )
+
+    def hop_half(way, slot, part_of):
+        at = buf.at[way, slot, half_rows(part_of)]
+        if part_of == 0:
+            sems = send.at[way, slot], recv.at[way, slot]
+        else:
+            sems = half_send.at[way, slot % units], half_recv.at[way, slot % units]
+        return remote(at, at, *sems, {"fsdp": left if way == 0 else right})
+
+    def hop_factor(way, slot):
+        return remote(
+            factor.at[way, slot],
+            factor.at[way, slot],
+            factor_send.at[way, slot],
+            factor_recv.at[way, slot],
+            {"fsdp": left if way == 0 else right},
+        )
+
+    def is_late(slot):
+        return slot // units == last - 2
+
+    def gossip(unit, part_of):
+        device = {"replica": partner}
+        rows = half_rows(part_of)
         return (
             remote(
-                buf.at[way, slot],
-                buf.at[way, slot],
-                send.at[way, slot],
-                recv.at[way, slot],
+                out_buf.at[unit, rows],
+                in_buf.at[unit, rows],
+                gossip_send.at[unit, part_of],
+                gossip_recv.at[unit, part_of],
                 device,
             ),
             remote(
-                factor.at[way, slot],
-                factor.at[way, slot],
-                factor_send.at[way, slot],
-                factor_recv.at[way, slot],
+                out_factor.at[unit, part_of],
+                in_factor.at[unit, part_of],
+                gossip_factor_send.at[unit, part_of],
+                gossip_factor_recv.at[unit, part_of],
                 device,
             ),
         )
 
-    def gossip(unit):
-        device = {"replica": partner}
-        return (
-            remote(
-                out_buf.at[unit],
-                in_buf.at[unit],
-                gossip_send.at[unit],
-                gossip_recv.at[unit],
-                device,
-            ),
-            remote(
-                out_factor.at[unit],
-                in_factor.at[unit],
-                gossip_factor_send.at[unit],
-                gossip_factor_recv.at[unit],
-                device,
-            ),
-        )
-
     def new_copy(unit):
         return pltpu.make_async_copy(new.at[unit], new_hbm.at[0, :, span(unit)], new_sem.at[unit])
 
-    def mixed_copy(unit):
+    def mixed_copy(unit, part_of):
+        rows = half_rows(part_of)
         return pltpu.make_async_copy(
-            mixed.at[unit], mixed_hbm.at[0, :, span(unit)], mixed_sem.at[unit]
+            mixed.at[unit, rows],
+            mixed_hbm.at[0, rows, span(unit)],
+            mixed_sem.at[unit, part_of],
         )
 
     order = []
@@ -312,8 +332,6 @@
         code = jnp.round(value * (TOP / largest * (1.0 - 1e-6)))
         return code.astype(jnp.int32).astype(jnp.int16), largest * (1.0 / TOP / (1.0 - 1e-6))
 
-    groups = [(g, slice(g * GROUP, (g + 1) * GROUP)) for g in range(features // GROUP)]
-
     def multiply(slot, target, rank, unit, with_edge):
         @pl.when(unit == 0)
         def _():
@@ -337,24 +355,27 @@
 
             part[slot] += dot(edge_tok[rank], edge_grad[unit])
 
-    def receive(slot, way, at):
-        for copy in hop(way, at):
-            copy.wait_recv()
-        for g, rows in groups:
-            part[slot, rows] += decode(buf[way, at, rows], factor[way, at, g : g + 1])
-
     def forward(way, at, beside_end):
         rank = at // units
         multiply(way, rank if way == 0 else last - rank, rank, at % units, beside_end)
 
         @pl.when(jnp.logical_not(beside_end))
         def _():
-            receive(way, way, at)
-
-        for g, rows in groups:
-            buf[way, at, rows], factor[way, at, g : g + 1] = encode(part[way, rows])
-        for copy in hop(way, at):
-            copy.start()
+            hop_factor(way, at).wait_recv()
+            hop_whole(way, at).wait_recv()
+            part[way] += decode(buf[way, at], factor[way, at])
+
+        buf[way, at], factor[way, at] = encode(part[way])
+        hop_factor(way, at).start()
+
+        @pl.when(is_late(at))
+        def _():
+            hop_half(way, at, 0).start()
+            hop_half(way, at, 1).start()
+
+        @pl.when(jnp.logical_not(is_late(at)))
+        def _():
+            hop_whole(way, at).start()
 
     from_right = chip * units
     from_left = (last - chip) * units
@@ -365,24 +386,38 @@
     def finish(unit):
         multiply(2, chip, last - 1, unit, next_to_end)
 
-        @pl.when(chip < last - 1)
-        def _():
-            receive(2, 0, jnp.minimum(from_right + unit, largest_slot))
-
-        @pl.when(chip > 1)
-        def _():
-            receive(2, 1, jnp.minimum(from_left + unit, largest_slot))
-
-        for copy in load(unit):
-            copy.wait()
-        for g, rows in groups:
+        for part_of in range(2):
+            rows = slice(part_of * half, (part_of + 1) * half)
+
+            for way, begin, there in ((0, from_right, chip < last - 1), (1, from_left, chip > 1)):
+
+                @pl.when(there)
+                def _(way=way, begin=begin):
+                    at = jnp.minimum(begin + unit, largest_slot)
+                    late = is_late(at)
+                    if part_of == 0:
+                        hop_factor(way, at).wait_recv()
+
+                        @pl.when(jnp.logical_not(late))
+                        def _():
+                            hop_whole(way, at).wait_recv()
+
+                    @pl.when(late)
+                    def _():
+                        hop_half(way, at, part_of).wait_recv()
+
+                    part[2, rows] += decode(buf[way, at, rows], factor[way, at])
+
+            if part_of == 0:
+                for copy in load(unit):
+                    copy.wait()
             moment = 0.9 * moments[unit, rows] + part[2, rows] * scale
             new[unit, rows] = moment
             value = weights[unit, rows].astype(jnp.float32) - 0.05 * moment
             updated[unit, rows] = value
-            out_buf[unit, rows], out_factor[unit, g : g + 1] = encode(value)
-        for copy in gossip(unit):
-            copy.start()
+            out_buf[unit, rows], out_factor[unit, part_of] = encode(value)
+            for copy in gossip(unit, part_of):
+                copy.start()
         new_copy(unit).start()
 
     begin_finish = jnp.maximum(
@@ -412,25 +447,36 @@
     steps = (last - 1) * max(units, HOP) + units + HOP
     lax.fori_loop(0, steps, step, 0)
 
-    def mix(unit, carry):
-        for copy in gossip(unit):
+    def mix(i, carry):
+        unit, part_of = i // 2, i % 2
+        for copy in gossip(unit, part_of):
             copy.wait_recv()
-        for g, rows in groups:
-            theirs = decode(in_buf[unit, rows], in_factor[unit, g : g + 1])
-            mixed[unit, rows] = ((updated[unit, rows] + theirs) * 0.5).astype(jnp.bfloat16)
-        mixed_copy(unit).start()
+        rows = half_rows(part_of)
+        theirs = decode(in_buf[unit, rows], in_factor[unit, part_of])
+        mixed[unit, rows] = ((updated[unit, rows] + theirs) * 0.5).astype(jnp.bfloat16)
+        mixed_copy(unit, part_of).start()
         return carry
 
-    lax.fori_loop(0, units, mix, 0)
+    lax.fori_loop(0, 2 * units, mix, 0)
+
+    def drain_way(way, at):
+        hop_factor(way, at).wait_send()
+
+        @pl.when(is_late(at))
+        def _():
+            hop_half(way, at, 0).wait_send()
+            hop_half(way, at, 1).wait_send()
+
+        @pl.when(jnp.logical_not(is_late(at)))
+        def _():
+            hop_whole(way, at).wait_send()
 
     def drain_left(at, carry):
-        for copy in hop(0, at):
-            copy.wait_send()
+        drain_way(0, at)
         return carry
 
     def drain_right(at, carry):
-        for copy in hop(1, at):
-            copy.wait_send()
+        drain_way(1, at)
         return carry
 
     lax.fori_loop(0, jnp.where(chip < last, from_right, 0), drain_left, 0)
@@ -458,10 +504,11 @@
             sibling_copy(target).wait_send()
 
     def drain(unit, carry):
-        for copy in gossip(unit):
-            copy.wait_send()
         new_copy(unit).wait()
-        mixed_copy(unit).wait()
+        for part_of in range(2):
+            for copy in gossip(unit, part_of):
+                copy.wait_send()
+            mixed_copy(unit, part_of).wait()
         return carry
 
     lax.fori_loop(0, units, drain, 0)
@@ -475,7 +522,6 @@
     features = weights.shape[1]
     width = min(LANES, columns)
     units = columns // width
-    groups = features // GROUP
     passed = (last - 1) * units
     dma = pltpu.SemaphoreType.DMA
     return pl.pallas_call(
@@ -492,7 +538,7 @@
             pltpu.VMEM((last, 2, held, features), jnp.bfloat16),
             pltpu.VMEM((units, 2, held, width), jnp.bfloat16),
             pltpu.VMEM((2, passed, features, width), jnp.int16),
-            pltpu.VMEM((2, passed, groups, width), jnp.float32),
+            pltpu.VMEM((2, passed, 1, width), jnp.float32),
             pltpu.VMEM((3, features, width), jnp.float32),
             pltpu.VMEM((units, features, width), jnp.bfloat16),
             pltpu.VMEM((units, features, width), jnp.float32),
@@ -500,9 +546,9 @@
             pltpu.VMEM((units, features, width), jnp.float32),
             pltpu.VMEM((units, features, width), jnp.bfloat16),
             pltpu.VMEM((units, features, width), jnp.int16),
-            pltpu.VMEM((units, groups, width), jnp.float32),
+            pltpu.VMEM((units, 2, 1, width), jnp.float32),
             pltpu.VMEM((units, features, width), jnp.int16),
-            pltpu.VMEM((units, groups, width), jnp.float32),
+            pltpu.VMEM((units, 2, 1, width), jnp.float32),
             dma((chips,)),
             dma((chips,)),
             dma((chips,)),
@@ -520,12 +566,14 @@
             dma((2, passed)),
             dma((2, passed)),
             dma((2, passed)),
-            dma((units,)),
-            dma((units,)),
-            dma((units,)),
-            dma((units,)),
-            dma((units,)),
-            dma((units,)),
+            dma((2, units)),
+            dma((2, units)),
+            dma((units, 2)),
+            dma((units, 2)),
+            dma((units, 2)),
+            dma((units, 2)),
+            dma((units,)),
+            dma((units, 2)),
         ],
         compiler_params=pltpu.CompilerParams(
             collective_id=level, has_side_effects=True, vmem_limit_bytes=44 * 1024 * 1024

time: 97.1 us -> 97.6 us (level); the launches traced: 97 us -> 98.5 us
  Pallas kernels: 93.9 us -> 95.2 us
    pallas_call x1, Pallas kernels: 93.9 us -> 95.2 us  [step_with(): pl.pallas_call(functools.partial(kernel, replicas, chips, 1 << level, flo...]
where the time goes in v1:
time: 97.6 us; the launch traced here: 98.5 us
  Pallas kernels  95.2 us (98%)
  local copies, waits for them, and re-layouts  1.77 us (2%)
  between operations  1.3 us (1%)
    pallas_call x1, Pallas kernels, step_with(): pl.pallas_call(functools.partial(kernel, replicas, chips, 1 << level, flo...  95.2 us

profile of v1, /device:TPU:64, one launch (start us, length us, event | category | flops | bytes accessed | tf_op | source)
XLA Modules:
  0.0 98.5 jit_solution(11522636613892383326)
XLA Ops:
  1.3 95.4 %conditional.1 = ((bf16[1,256,1024]{2,1,0:T(8,128)(2,1)S(1)}, f32[1,256,1024]{2,1,0:T(8,128)S(1)})) conditional(s32[]{:T(128)} %clamp.3, (bf16[192,4096]{1,0:T(8,128)(2,1)}, bf16[192,1024]{1,0:T(8,128)(2,1)}, bf16[1,256,1024]{2,1,0:T(8,128)(2,1)}, f32[1,256,1024]{2,1,0:T(8,128)}) %tuple.22, ...), branch_computations={%region_0.1_spmd, %region_1.2_spmd, %region_2.3_spmd, %region_3.4_... | conditional | flops 1610612736 | bytes 4194312 | solution.py:598
  1.3 95.2 %branch_1_fun.1 = (bf16[1,256,1024]{2,1,0:T(8,128)(2,1)S(1)}, f32[1,256,1024]{2,1,0:T(8,128)S(1)}) custom-call(bf16[192,4096]{1,0:T(8,128)(2,1)} %get-tuple-element.44.tokens_hbm, bf16[192,1024]{1,0:T(8,128)(2,1)} %get-tuple-element.45.grads_hbm, bf16[1,256,1024]{2,1,0:T(8,128)(2,1)} %get-tuple-element.46.weights_hbm, ...), custom_call_target="tpu_custom_call" | custom-call | flops 1610612736 | bytes 4194304 | tf_op jit(solution)/shard_map/cond/branch_1_fun/pallas_call | solution.py:527
  96.7 0.8 copy.30
  97.5 1.0 copy.31
